TPU v7x, 32 devices: a whole 2x2x4 slice. The times are simulated.
32 devices in a mesh: pair: 4 (over z), dof: 8 (over y, x, core).
Axes of the slice: x: 2, y: 2, z: 4, core: 2. Of those that a mesh axis runs over, the one named last changes fastest.
Arguments:
- snapshots: float32 [128, 65536], P('pair', 'dof'), may hold values from -600 to 600
Outputs:
- rotated: float32 [128, 65536], P('pair', 'dof')
All inputs are finite; a program needn't handle non-finite values.
Results may differ from a plain program's by a relative error of at most 0.0003.
Values sent between devices are 32-bit elements; how exact they have to be, the bound alone decides.
A program may use at most 64 MiB of HBM per device.

v0:
```python
import jax
import jax.numpy as jnp
from jax import lax
from jax.sharding import PartitionSpec as P

STEPS = 4
SWEEPS = 2
highest = lax.Precision.HIGHEST


def passed_along(block, axis, distance):
    devices = range(lax.axis_size(axis))
    route = [(i - distance, i) for i in devices if i - distance in devices]
    return lax.ppermute(block, axis, route)


def jacobi(gram_matrix):
    pair_order = gram_matrix.shape[0]
    circle_size = pair_order - 1
    index_row = lax.broadcasted_iota(jnp.int32, (pair_order, pair_order), 0)
    index_col = lax.broadcasted_iota(jnp.int32, (pair_order, pair_order), 1)
    identity_mask = index_row == index_col
    upper_side = index_row < index_col
    indices = jnp.arange(pair_order, dtype=jnp.int32)

    def one_round(round_index, carried):
        gram_now, basis = carried
        shifted = (round_index % circle_size).astype(jnp.int32)
        mirror = (2 * shifted - indices + 2 * circle_size) % circle_size
        partner = jnp.where(
            indices == circle_size, shifted, jnp.where(indices == shifted, circle_size, mirror)
        )
        partner_mask = index_col == partner[:, None]
        zeros = jnp.zeros_like(gram_now)
        upper_part = jnp.where(upper_side, gram_now, gram_now.T)
        coupling = jnp.sum(jnp.where(partner_mask, upper_part, zeros), axis=1)
        own_diag = jnp.sum(jnp.where(identity_mask, gram_now, zeros), axis=1)
        other_diag = jnp.sum(jnp.where(partner_mask, own_diag[None, :] + zeros, zeros), axis=1)
        is_lower = indices < partner
        diag_lower = jnp.where(is_lower, own_diag, other_diag)
        diag_upper = jnp.where(is_lower, other_diag, own_diag)
        spread_diag = diag_upper - diag_lower
        orient = jnp.where(spread_diag >= 0, 1.0, -1.0).astype(jnp.float32)
        tangent = (
            orient
            * 2.0
            * coupling
            / (
                jnp.abs(spread_diag)
                + jnp.sqrt(spread_diag * spread_diag + 4.0 * coupling * coupling)
            )
        )
        cosine = 1.0 / jnp.sqrt(1.0 + tangent * tangent)
        sine_part = cosine * tangent
        signed_sine = jnp.where(is_lower, sine_part, -sine_part)
        rotation = jnp.where(
            identity_mask,
            cosine[:, None] + zeros,
            jnp.where(partner_mask, signed_sine[:, None] + zeros, zeros),
        )
        gram_now = jnp.dot(
            jnp.dot(rotation.T, gram_now, precision=highest), rotation, precision=highest
        )
        basis = jnp.dot(basis, rotation, precision=highest)
        return (gram_now, basis)

    start = (gram_matrix, jnp.eye(pair_order, dtype=jnp.float32))
    final_gram, basis = lax.fori_loop(0, SWEEPS * circle_size, one_round, start)
    return basis


def body(snapshots):
    pair_order = snapshots.shape[0]
    half_order = pair_order // 2
    device_place = lax.axis_index("pair")
    final_place = lax.axis_size("pair") - 1
    is_first = device_place == 0
    is_last = device_place == final_place
    pair_rows = snapshots
    for step_index in range(STEPS):
        local_gram = jnp.dot(pair_rows, pair_rows.T, precision=highest)
        gram_matrix = lax.psum(local_gram, "dof")
        turned = jacobi(gram_matrix)
        moved = jnp.dot(turned.T, pair_rows, precision=highest)
        new_top = moved[:half_order]
        new_low = moved[half_order:]
        rising = jnp.where(is_first, new_low, new_top)
        got_rising = passed_along(rising, "pair", 1)
        got_falling = passed_along(new_low, "pair", -1)
        next_top = jnp.where(is_first, new_top, got_rising)
        next_low = jnp.where(is_last, new_top, got_falling)
        pair_rows = jnp.concatenate([next_top, next_low], axis=0)
    return pair_rows


def solution(mesh):
    in_specs = (P("pair", "dof"),)
    out_specs = P("pair", "dof")
    return jax.shard_map(body, mesh=mesh, in_specs=in_specs, out_specs=out_specs, check_vma=False)
```

profile of v0, /device:TPU:0, one launch (start us, length us, event | category | flops | bytes accessed | tf_op | source)
XLA Modules:
  0.0 519.9 jit_solution(5323736316995581943)
XLA Ops:
  0.0 0.6 copy-done.1
  0.6 0.6 copy-done
  1.2 1.0 fusion.185
  2.2 25.5 %psum.28 = f32[32,32]{1,0:T(8,128)S(1)} all-reduce(f32[32,32]{1,0:T(8,128)S(1)} %fusion.185), channel_id=1, replica_groups=mesh['pair'=4,'dof'=8] {'dof'}, use_global_device_ids=true, to_apply=%region_0.0 | all-reduce | flops 1024 | bytes 8192 | tf_op jit(solution)/shard_map/psum | solution.py:82
  27.7 85.2 %while.76 = (s32[]{:T(128)}, f32[32,32]{1,0:T(8,128)S(1)}, f32[32,32]{0,1:T(8,128)S(1)}, s32[]{:T(128)}, s32[]{:T(128)}, /*index=5*/s32[]{:T(128)}, s32[]{:T(128)}) while((s32[]{:T(128)}, f32[32,32]{1,0:T(8,128)S(1)}, f32[32,32]{0,1:T(8,128)S(1)}, s32[]{:T(128)}, s32[]{:T(128)}, /*index=5*/s32[]{:T(128)}, ...), condition=%wide.region_5.6_spmd.clone.clone, body=%wide.region_1.5_spmd.clone.clone.sunk | while | flops 1205001 | bytes 52267 | solution.py:68
  32.4 0.3 convolution_bitcast_fusion.8
  32.7 0.3 fusion.254
  33.8 0.3 convolution_bitcast_fusion.8
  34.1 0.3 fusion.254
  112.9 1.0 fusion.186
  113.9 0.9 slice_select_fusion.11
  114.8 3.5 collective-permute-start
  118.3 1.3 collective-permute-start.1
  119.6 7.6 %collective-permute-done = f32[16,8192]{1,0:T(8,128)S(1)} collective-permute-done((f32[16,8192]{1,0:T(8,128)}, f32[16,8192]{1,0:T(8,128)S(1)}, u32[]{:S(2)}, u32[]{:S(2)}) %collective-permute-start) | collective-permute-done | bytes 524320 | tf_op jit(solution)/shard_map/ppermute | solution.py:14
  127.2 0.8 copy-done.6
  128.0 3.1 collective-permute-done.1
  131.2 1.1 slice_select_fusion.10
  132.3 1.0 fusion.173
  133.3 24.1 %psum.29 = f32[32,32]{1,0:T(8,128)S(1)} all-reduce(f32[32,32]{1,0:T(8,128)S(1)} %fusion.173), channel_id=1, replica_groups=mesh['pair'=4,'dof'=8] {'dof'}, use_global_device_ids=true, to_apply=%region_6.7 | all-reduce | flops 1024 | bytes 8192 | tf_op jit(solution)/shard_map/psum | solution.py:82
  157.4 85.2 %while.77 = (s32[]{:T(128)}, f32[32,32]{1,0:T(8,128)S(1)}, f32[32,32]{0,1:T(8,128)S(1)}, s32[]{:T(128)}, s32[]{:T(128)}, /*index=5*/s32[]{:T(128)}, s32[]{:T(128)}) while((s32[]{:T(128)}, f32[32,32]{1,0:T(8,128)S(1)}, f32[32,32]{0,1:T(8,128)S(1)}, s32[]{:T(128)}, s32[]{:T(128)}, /*index=5*/s32[]{:T(128)}, ...), condition=%wide.region_11.12_spmd.clone.clone, body=%wide.region_7.11_spmd.clone.clone.sunk | while | flops 1205001 | bytes 52267 | solution.py:68
  242.6 1.0 fusion.172
  243.6 0.9 slice_select_fusion.8
  244.4 3.6 collective-permute-start.2
  248.1 1.3 collective-permute-start.3
  249.4 7.6 %collective-permute-done.2 = f32[16,8192]{1,0:T(8,128)S(1)} collective-permute-done((f32[16,8192]{1,0:T(8,128)}, f32[16,8192]{1,0:T(8,128)S(1)}, u32[]{:S(2)}, u32[]{:S(2)}) %collective-permute-start.2) | collective-permute-done | bytes 524320 | tf_op jit(solution)/shard_map/ppermute | solution.py:14
  257.0 0.8 copy-done.7
  257.8 3.1 collective-permute-done.3
  260.9 1.1 slice_select_fusion.7
  262.1 1.0 fusion.171
  263.0 24.2 %psum.30 = f32[32,32]{1,0:T(8,128)S(1)} all-reduce(f32[32,32]{1,0:T(8,128)S(1)} %fusion.171), channel_id=1, replica_groups=mesh['pair'=4,'dof'=8] {'dof'}, use_global_device_ids=true, to_apply=%region_12.13 | all-reduce | flops 1024 | bytes 8192 | tf_op jit(solution)/shard_map/psum | solution.py:82
  287.2 85.2 %while.78 = (s32[]{:T(128)}, f32[32,32]{1,0:T(8,128)S(1)}, f32[32,32]{0,1:T(8,128)S(1)}, s32[]{:T(128)}, s32[]{:T(128)}, /*index=5*/s32[]{:T(128)}, s32[]{:T(128)}) while((s32[]{:T(128)}, f32[32,32]{1,0:T(8,128)S(1)}, f32[32,32]{0,1:T(8,128)S(1)}, s32[]{:T(128)}, s32[]{:T(128)}, /*index=5*/s32[]{:T(128)}, ...), condition=%wide.region_17.18_spmd.clone.clone, body=%wide.region_13.17_spmd.clone.clone.sunk | while | flops 1205001 | bytes 52267 | solution.py:68
  372.4 1.0 fusion.170
  373.5 0.9 slice_select_fusion.5
  374.3 3.6 collective-permute-start.4
  378.0 1.3 collective-permute-start.5
  379.3 7.6 %collective-permute-done.4 = f32[16,8192]{1,0:T(8,128)S(1)} collective-permute-done((f32[16,8192]{1,0:T(8,128)}, f32[16,8192]{1,0:T(8,128)S(1)}, u32[]{:S(2)}, u32[]{:S(2)}) %collective-permute-start.4) | collective-permute-done | bytes 524320 | tf_op jit(solution)/shard_map/ppermute | solution.py:14
  386.9 0.8 copy-done.8
  387.7 3.1 collective-permute-done.5
  390.8 1.1 slice_select_fusion.4
  391.9 1.0 fusion.169
  392.9 24.2 %psum.31 = f32[32,32]{1,0:T(8,128)S(1)} all-reduce(f32[32,32]{1,0:T(8,128)S(1)} %fusion.169), channel_id=1, replica_groups=mesh['pair'=4,'dof'=8] {'dof'}, use_global_device_ids=true, to_apply=%region_18.19 | all-reduce | flops 1024 | bytes 8192 | tf_op jit(solution)/shard_map/psum | solution.py:82
  417.1 85.2 %while.79 = (s32[]{:T(128)}, f32[32,32]{1,0:T(8,128)S(1)}, f32[32,32]{0,1:T(8,128)S(1)}, s32[]{:T(128)}, s32[]{:T(128)}, /*index=5*/s32[]{:T(128)}, s32[]{:T(128)}) while((s32[]{:T(128)}, f32[32,32]{1,0:T(8,128)S(1)}, f32[32,32]{0,1:T(8,128)S(1)}, s32[]{:T(128)}, s32[]{:T(128)}, /*index=5*/s32[]{:T(128)}, ...), condition=%wide.region_23.24_spmd.clone.clone, body=%wide.region_19.23_spmd.clone.clone.sunk | while | flops 1205001 | bytes 52267 | solution.py:68
  502.3 1.0 fusion.168
  503.4 2.6 collective-permute-start.6
  506.1 1.3 collective-permute-start.7
  507.4 7.3 %collective-permute-done.6 = f32[16,8192]{1,0:T(8,128)S(1)} collective-permute-done((f32[16,8192]{1,0:T(8,128)S(1)}, f32[16,8192]{1,0:T(8,128)S(1)}, u32[]{:S(2)}, u32[]{:S(2)}) %collective-permute-start.6) | collective-permute-done | bytes 524320 | tf_op jit(solution)/shard_map/ppermute | solution.py:14
  514.7 4.1 collective-permute-done.7
  518.9 1.0 pad_maximum_fusion.3
  (2492 shorter events, 317.5 us)
Async XLA Ops:
  0.0 1.2 copy-start
  0.0 0.6 copy-start.1
  2.2 25.5 %copy-start.3 = (f32[32,32]{0,1:T(8,128)S(1)}, f32[32,32]{0,1:T(8,128)}, u32[]{:S(2)}) copy-start(f32[32,32]{0,1:T(8,128)} %copy-done.1) | copy-start | bytes 12292
  114.8 12.4 %collective-permute-start = (f32[16,8192]{1,0:T(8,128)}, f32[16,8192]{1,0:T(8,128)S(1)}, u32[]{:S(2)}, u32[]{:S(2)}) collective-permute-start(f32[16,8192]{1,0:T(8,128)} %get-tuple-element.955), channel_id=1, source_target_pairs={{0,8},{8,16},{16,24},{1,9},{9,17},{17,25},{2,10},{10,18},{18,26},{... | collective-permute-start | bytes 1572872 | tf_op jit(solution)/shard_map/ppermute | solution.py:14
  118.3 12.9 %collective-permute-start.1 = (f32[16,8192]{1,0:T(8,128)S(1)}, f32[16,8192]{1,0:T(8,128)}, u32[]{:S(2)}, u32[]{:S(2)}) collective-permute-start(f32[16,8192]{1,0:T(8,128)S(1)} %get-tuple-element.956), channel_id=1, source_target_pairs={{8,0},{16,8},{24,16},{9,1},{17,9},{25,17},{10,2},{18,10},{26,18},{... | collective-permute-start | bytes 1572872 | tf_op jit(solution)/shard_map/ppermute | solution.py:14
  127.2 0.8 copy-start.6
  133.3 24.1 %copy-start.4 = (f32[32,32]{0,1:T(8,128)S(1)}, f32[32,32]{0,1:T(8,128)}, u32[]{:S(2)}) copy-start(f32[32,32]{0,1:T(8,128)} %copy-done.1) | copy-start | bytes 12292
  244.4 12.6 %collective-permute-start.2 = (f32[16,8192]{1,0:T(8,128)}, f32[16,8192]{1,0:T(8,128)S(1)}, u32[]{:S(2)}, u32[]{:S(2)}) collective-permute-start(f32[16,8192]{1,0:T(8,128)} %get-tuple-element.951), channel_id=1, source_target_pairs={{0,8},{8,16},{16,24},{1,9},{9,17},{17,25},{2,10},{10,18},{18,26},{... | collective-permute-start | bytes 1572872 | tf_op jit(solution)/shard_map/ppermute | solution.py:14
  248.1 12.9 %collective-permute-start.3 = (f32[16,8192]{1,0:T(8,128)S(1)}, f32[16,8192]{1,0:T(8,128)}, u32[]{:S(2)}, u32[]{:S(2)}) collective-permute-start(f32[16,8192]{1,0:T(8,128)S(1)} %get-tuple-element.952), channel_id=1, source_target_pairs={{8,0},{16,8},{24,16},{9,1},{17,9},{25,17},{10,2},{18,10},{26,18},{... | collective-permute-start | bytes 1572872 | tf_op jit(solution)/shard_map/ppermute | solution.py:14
  257.0 0.8 copy-start.7
  263.0 24.2 %copy-start.5 = (f32[32,32]{0,1:T(8,128)S(1)}, f32[32,32]{0,1:T(8,128)}, u32[]{:S(2)}) copy-start(f32[32,32]{0,1:T(8,128)} %copy-done.1) | copy-start | bytes 12292
  374.3 12.6 %collective-permute-start.4 = (f32[16,8192]{1,0:T(8,128)}, f32[16,8192]{1,0:T(8,128)S(1)}, u32[]{:S(2)}, u32[]{:S(2)}) collective-permute-start(f32[16,8192]{1,0:T(8,128)} %get-tuple-element.947), channel_id=1, source_target_pairs={{0,8},{8,16},{16,24},{1,9},{9,17},{17,25},{2,10},{10,18},{18,26},{... | collective-permute-start | bytes 1572872 | tf_op jit(solution)/shard_map/ppermute | solution.py:14
  378.0 12.9 %collective-permute-start.5 = (f32[16,8192]{1,0:T(8,128)S(1)}, f32[16,8192]{1,0:T(8,128)}, u32[]{:S(2)}, u32[]{:S(2)}) collective-permute-start(f32[16,8192]{1,0:T(8,128)S(1)} %get-tuple-element.948), channel_id=1, source_target_pairs={{8,0},{16,8},{24,16},{9,1},{17,9},{25,17},{10,2},{18,10},{26,18},{... | collective-permute-start | bytes 1572872 | tf_op jit(solution)/shard_map/ppermute | solution.py:14
  386.9 0.8 copy-start.8
  392.9 24.2 %copy-start.2 = (f32[32,32]{0,1:T(8,128)S(1)}, f32[32,32]{0,1:T(8,128)}, u32[]{:S(2)}) copy-start(f32[32,32]{0,1:T(8,128)} %copy-done.1) | copy-start | bytes 12292
  503.4 11.2 %collective-permute-start.6 = (f32[16,8192]{1,0:T(8,128)S(1)}, f32[16,8192]{1,0:T(8,128)S(1)}, u32[]{:S(2)}, u32[]{:S(2)}) collective-permute-start(f32[16,8192]{1,0:T(8,128)S(1)} %get-tuple-element.943), channel_id=1, source_target_pairs={{0,8},{8,16},{16,24},{1,9},{9,17},{17,25},{2,10},{10,18},{18,26},{... | collective-permute-start | bytes 1572872 | tf_op jit(solution)/shard_map/ppermute | solution.py:14
  506.1 12.7 %collective-permute-start.7 = (f32[16,8192]{1,0:T(8,128)S(1)}, f32[16,8192]{1,0:T(8,128)S(1)}, u32[]{:S(2)}, u32[]{:S(2)}) collective-permute-start(f32[16,8192]{1,0:T(8,128)S(1)} %get-tuple-element.944), channel_id=1, source_target_pairs={{8,0},{16,8},{24,16},{9,1},{17,9},{25,17},{10,2},{18,10},{26,18},{... | collective-permute-start | bytes 1572872 | tf_op jit(solution)/shard_map/ppermute | solution.py:14
where the time goes:
time: 521 us; the launch traced here: 520 us
  matrix products  200 us (38%)
  other arithmetic  115 us (22%)
  blocking collectives  97.9 us (19%)
  waiting for transfers between devices  43.7 us (8%)
  loops' own time  22.4 us (4%)
  local copies, waits for them, and re-layouts  22.1 us (4%)
  starting transfers between devices  18.5 us (4%)
    psum x4, blocking collectives, body(): gram_matrix = lax.psum(local_gram, 'dof')  97.9 us
    dot_general x248, matrix products, one_round(): basis = jnp.dot(basis, rotation, precision=highest)  69.6 us
    dot_general x248, matrix products, one_round(): jnp.dot(rotation.T, gram_now, precision=highest)  69.6 us
    dot_general x248, matrix products, one_round(): jnp.dot(jnp.dot(rotation.T, gram_now, precision=highest), rotation, preci...  52.7 us
    reduce_sum x248, other arithmetic, one_round(): jnp.sum(jnp.where(partner_mask, own_diag[None, :] + zeros, zeros), axis=1)  44.4 us
    ppermute x8, waiting for transfers between devices, passed_along(): return lax.ppermute(block, axis, route)  43.7 us
    reduce_sum x248, other arithmetic, one_round(): own_diag = jnp.sum(jnp.where(identity_mask, gram_now, zeros), axis=1)  43.6 us
    another operation x4, loops' own time, jacobi(): final_gram, basis = lax.fori_loop(0, SWEEPS * circle_size, one_round, start)  22.4 us
  transfers between devices with their start and end apart: 8, of which 8 were waited for; matrix products, arithmetic and copies ran while one was open for 0% of the time, Pallas kernels for 0%

commit v1 on v0

--- a/solution.py
+++ b/solution.py
@@ -79,7 +79,7 @@
     pair_rows = snapshots
     for step_index in range(STEPS):
         local_gram = jnp.dot(pair_rows, pair_rows.T, precision=highest)
-        gram_matrix = lax.psum(local_gram, "dof")
+        gram_matrix = jnp.sum(lax.all_gather(local_gram, "dof"), axis=0)
         turned = jacobi(gram_matrix)
         moved = jnp.dot(turned.T, pair_rows, precision=highest)
         new_top = moved[:half_order]

time: 521 us -> 475 us (0.912)
  blocking collectives: 97.9 us -> 37.5 us
  waiting for transfers between devices: 43.7 us -> 55.9 us
    psum x4 -> x0, blocking collectives: 97.9 us -> none  [body(): gram_matrix = lax.psum(local_gram, 'dof')]
    all_gather x0 -> x4, blocking collectives: none -> 37.5 us  [body(): gram_matrix = jnp.sum(lax.all_gather(local_gram, 'dof'), axis=0)]
    ppermute x8, waiting for transfers between devices: 43.7 us -> 55.9 us  [passed_along(): return lax.ppermute(block, axis, route)]
where the time goes in v1:
time: 475 us; the launch traced here: 474 us
  matrix products  200 us (42%)
  other arithmetic  115 us (24%)
  waiting for transfers between devices  55.9 us (12%)
  blocking collectives  37.5 us (8%)
  local copies, waits for them, and re-layouts  24.9 us (5%)
  loops' own time  22.3 us (5%)
  starting transfers between devices  18.3 us (4%)
    dot_general x248, matrix products, one_round(): basis = jnp.dot(basis, rotation, precision=highest)  69.6 us
    dot_general x248, matrix products, one_round(): jnp.dot(rotation.T, gram_now, precision=highest)  69.6 us
    ppermute x8, waiting for transfers between devices, passed_along(): return lax.ppermute(block, axis, route)  55.9 us
    dot_general x248, matrix products, one_round(): jnp.dot(jnp.dot(rotation.T, gram_now, precision=highest), rotation, preci...  52.7 us
    reduce_sum x248, other arithmetic, one_round(): jnp.sum(jnp.where(partner_mask, own_diag[None, :] + zeros, zeros), axis=1)  44.4 us
    reduce_sum x248, other arithmetic, one_round(): own_diag = jnp.sum(jnp.where(identity_mask, gram_now, zeros), axis=1)  43.6 us
    all_gather x4, blocking collectives, body(): gram_matrix = jnp.sum(lax.all_gather(local_gram, 'dof'), axis=0)  37.5 us
    another operation x4, loops' own time, jacobi(): final_gram, basis = lax.fori_loop(0, SWEEPS * circle_size, one_round, start)  22.3 us
  transfers between devices with their start and end apart: 8, of which 8 were waited for; matrix products, arithmetic and copies ran while one was open for 0% of the time, Pallas kernels for 0%

profile of v1, /device:TPU:0, one launch (start us, length us, event | category | flops | bytes accessed | tf_op | source)
XLA Modules:
  0.0 474.2 jit_solution(15124073660135748610)
XLA Ops:
  0.0 0.6 copy-done.1
  0.6 0.6 copy-done
  1.2 1.0 fusion.185
  2.2 10.7 %all-gather = f32[256,32]{1,0:T(8,128)S(1)} all-gather(f32[32,32]{1,0:T(8,128)S(1)} %fusion.185), channel_id=2, replica_groups=mesh['pair'=4,'dof'=8] {'dof'}, dimensions={0}, use_global_device_ids=true | all-gather | bytes 36864 | tf_op jit(solution)/shard_map/all_gather | solution.py:82
  12.9 0.7 copy-done.3
  13.6 85.2 %while.76 = (s32[]{:T(128)}, f32[32,32]{1,0:T(8,128)S(1)}, f32[32,32]{0,1:T(8,128)S(1)}, s32[]{:T(128)}, s32[]{:T(128)}, /*index=5*/s32[]{:T(128)}, s32[]{:T(128)}) while((s32[]{:T(128)}, f32[32,32]{1,0:T(8,128)S(1)}, f32[32,32]{0,1:T(8,128)S(1)}, s32[]{:T(128)}, s32[]{:T(128)}, /*index=5*/s32[]{:T(128)}, ...), condition=%wide.region_5.6_spmd.clone.clone, body=%wide.region_1.5_spmd.clone.clone.sunk | while | flops 1205001 | bytes 52267 | solution.py:68
  98.8 1.0 fusion.186
  99.8 0.9 slice_select_fusion.11
  100.7 3.5 collective-permute-start
  104.2 1.3 collective-permute-start.1
  105.5 10.6 %collective-permute-done = f32[16,8192]{1,0:T(8,128)S(1)} collective-permute-done((f32[16,8192]{1,0:T(8,128)}, f32[16,8192]{1,0:T(8,128)S(1)}, u32[]{:S(2)}, u32[]{:S(2)}) %collective-permute-start) | collective-permute-done | bytes 524320 | tf_op jit(solution)/shard_map/ppermute | solution.py:14
  116.1 0.8 copy-done.6
  116.9 3.1 collective-permute-done.1
  120.1 1.1 slice_select_fusion.10
  121.2 1.0 fusion.173
  122.2 9.2 %all-gather.1 = f32[256,32]{1,0:T(8,128)S(1)} all-gather(f32[32,32]{1,0:T(8,128)S(1)} %fusion.173), channel_id=3, replica_groups=mesh['pair'=4,'dof'=8] {'dof'}, dimensions={0}, use_global_device_ids=true | all-gather | bytes 36864 | tf_op jit(solution)/shard_map/all_gather | solution.py:82
  131.4 0.7 copy-done.4
  132.1 85.2 %while.77 = (s32[]{:T(128)}, f32[32,32]{1,0:T(8,128)S(1)}, f32[32,32]{0,1:T(8,128)S(1)}, s32[]{:T(128)}, s32[]{:T(128)}, /*index=5*/s32[]{:T(128)}, s32[]{:T(128)}) while((s32[]{:T(128)}, f32[32,32]{1,0:T(8,128)S(1)}, f32[32,32]{0,1:T(8,128)S(1)}, s32[]{:T(128)}, s32[]{:T(128)}, /*index=5*/s32[]{:T(128)}, ...), condition=%wide.region_11.12_spmd.clone.clone, body=%wide.region_7.11_spmd.clone.clone.sunk | while | flops 1205001 | bytes 52267 | solution.py:68
  217.3 1.0 fusion.172
  218.3 0.9 slice_select_fusion.8
  219.2 3.6 collective-permute-start.2
  222.8 1.3 collective-permute-start.3
  224.1 10.7 %collective-permute-done.2 = f32[16,8192]{1,0:T(8,128)S(1)} collective-permute-done((f32[16,8192]{1,0:T(8,128)}, f32[16,8192]{1,0:T(8,128)S(1)}, u32[]{:S(2)}, u32[]{:S(2)}) %collective-permute-start.2) | collective-permute-done | bytes 524320 | tf_op jit(solution)/shard_map/ppermute | solution.py:14
  234.8 0.8 copy-done.7
  235.6 3.1 collective-permute-done.3
  238.7 1.1 slice_select_fusion.7
  239.8 1.0 fusion.171
  240.8 8.3 %all-gather.2 = f32[256,32]{1,0:T(8,128)S(1)} all-gather(f32[32,32]{1,0:T(8,128)S(1)} %fusion.171), channel_id=4, replica_groups=mesh['pair'=4,'dof'=8] {'dof'}, dimensions={0}, use_global_device_ids=true | all-gather | bytes 36864 | tf_op jit(solution)/shard_map/all_gather | solution.py:82
  249.1 0.7 copy-done.5
  249.8 85.2 %while.78 = (s32[]{:T(128)}, f32[32,32]{1,0:T(8,128)S(1)}, f32[32,32]{0,1:T(8,128)S(1)}, s32[]{:T(128)}, s32[]{:T(128)}, /*index=5*/s32[]{:T(128)}, s32[]{:T(128)}) while((s32[]{:T(128)}, f32[32,32]{1,0:T(8,128)S(1)}, f32[32,32]{0,1:T(8,128)S(1)}, s32[]{:T(128)}, s32[]{:T(128)}, /*index=5*/s32[]{:T(128)}, ...), condition=%wide.region_17.18_spmd.clone.clone, body=%wide.region_13.17_spmd.clone.clone.sunk | while | flops 1205001 | bytes 52267 | solution.py:68
  335.0 1.0 fusion.170
  336.0 0.9 slice_select_fusion.5
  336.9 3.6 collective-permute-start.4
  340.5 1.3 collective-permute-start.5
  341.8 10.7 %collective-permute-done.4 = f32[16,8192]{1,0:T(8,128)S(1)} collective-permute-done((f32[16,8192]{1,0:T(8,128)}, f32[16,8192]{1,0:T(8,128)S(1)}, u32[]{:S(2)}, u32[]{:S(2)}) %collective-permute-start.4) | collective-permute-done | bytes 524320 | tf_op jit(solution)/shard_map/ppermute | solution.py:14
  352.5 0.8 copy-done.8
  353.3 3.1 collective-permute-done.5
  356.4 1.1 slice_select_fusion.4
  357.5 1.0 fusion.169
  358.5 9.4 %all-gather.3 = f32[256,32]{1,0:T(8,128)S(1)} all-gather(f32[32,32]{1,0:T(8,128)S(1)} %fusion.169), channel_id=5, replica_groups=mesh['pair'=4,'dof'=8] {'dof'}, dimensions={0}, use_global_device_ids=true | all-gather | bytes 36864 | tf_op jit(solution)/shard_map/all_gather | solution.py:82
  367.9 0.7 copy-done.2
  368.6 85.2 %while.79 = (s32[]{:T(128)}, f32[32,32]{1,0:T(8,128)S(1)}, f32[32,32]{0,1:T(8,128)S(1)}, s32[]{:T(128)}, s32[]{:T(128)}, /*index=5*/s32[]{:T(128)}, s32[]{:T(128)}) while((s32[]{:T(128)}, f32[32,32]{1,0:T(8,128)S(1)}, f32[32,32]{0,1:T(8,128)S(1)}, s32[]{:T(128)}, s32[]{:T(128)}, /*index=5*/s32[]{:T(128)}, ...), condition=%wide.region_23.24_spmd.clone.clone, body=%wide.region_19.23_spmd.clone.clone.sunk | while | flops 1205001 | bytes 52267 | solution.py:68
  453.8 1.0 fusion.168
  454.9 2.4 collective-permute-start.6
  457.3 1.3 collective-permute-start.7
  458.6 10.3 %collective-permute-done.6 = f32[16,8192]{1,0:T(8,128)S(1)} collective-permute-done((f32[16,8192]{1,0:T(8,128)S(1)}, f32[16,8192]{1,0:T(8,128)S(1)}, u32[]{:S(2)}, u32[]{:S(2)}) %collective-permute-start.6) | collective-permute-done | bytes 524320 | tf_op jit(solution)/shard_map/ppermute | solution.py:14
  468.9 4.1 collective-permute-done.7
  473.1 1.0 pad_maximum_fusion.3
  (2496 shorter events, 318.7 us)
Async XLA Ops:
  0.0 1.2 copy-start
  0.0 0.6 copy-start.1
  12.9 0.7 copy-start.3
  100.7 15.5 %collective-permute-start = (f32[16,8192]{1,0:T(8,128)}, f32[16,8192]{1,0:T(8,128)S(1)}, u32[]{:S(2)}, u32[]{:S(2)}) collective-permute-start(f32[16,8192]{1,0:T(8,128)} %get-tuple-element.955), channel_id=1, source_target_pairs={{0,8},{8,16},{16,24},{1,9},{9,17},{17,25},{2,10},{10,18},{18,26},{... | collective-permute-start | bytes 1572872 | tf_op jit(solution)/shard_map/ppermute | solution.py:14
  104.2 15.9 %collective-permute-start.1 = (f32[16,8192]{1,0:T(8,128)S(1)}, f32[16,8192]{1,0:T(8,128)}, u32[]{:S(2)}, u32[]{:S(2)}) collective-permute-start(f32[16,8192]{1,0:T(8,128)S(1)} %get-tuple-element.956), channel_id=1, source_target_pairs={{8,0},{16,8},{24,16},{9,1},{17,9},{25,17},{10,2},{18,10},{26,18},{... | collective-permute-start | bytes 1572872 | tf_op jit(solution)/shard_map/ppermute | solution.py:14
  116.1 0.8 copy-start.6
  131.4 0.7 copy-start.4
  219.2 15.6 %collective-permute-start.2 = (f32[16,8192]{1,0:T(8,128)}, f32[16,8192]{1,0:T(8,128)S(1)}, u32[]{:S(2)}, u32[]{:S(2)}) collective-permute-start(f32[16,8192]{1,0:T(8,128)} %get-tuple-element.951), channel_id=1, source_target_pairs={{0,8},{8,16},{16,24},{1,9},{9,17},{17,25},{2,10},{10,18},{18,26},{... | collective-permute-start | bytes 1572872 | tf_op jit(solution)/shard_map/ppermute | solution.py:14
  222.8 15.9 %collective-permute-start.3 = (f32[16,8192]{1,0:T(8,128)S(1)}, f32[16,8192]{1,0:T(8,128)}, u32[]{:S(2)}, u32[]{:S(2)}) collective-permute-start(f32[16,8192]{1,0:T(8,128)S(1)} %get-tuple-element.952), channel_id=1, source_target_pairs={{8,0},{16,8},{24,16},{9,1},{17,9},{25,17},{10,2},{18,10},{26,18},{... | collective-permute-start | bytes 1572872 | tf_op jit(solution)/shard_map/ppermute | solution.py:14
  234.8 0.8 copy-start.7
  249.1 0.7 copy-start.5
  336.9 15.6 %collective-permute-start.4 = (f32[16,8192]{1,0:T(8,128)}, f32[16,8192]{1,0:T(8,128)S(1)}, u32[]{:S(2)}, u32[]{:S(2)}) collective-permute-start(f32[16,8192]{1,0:T(8,128)} %get-tuple-element.947), channel_id=1, source_target_pairs={{0,8},{8,16},{16,24},{1,9},{9,17},{17,25},{2,10},{10,18},{18,26},{... | collective-permute-start | bytes 1572872 | tf_op jit(solution)/shard_map/ppermute | solution.py:14
  340.5 15.9 %collective-permute-start.5 = (f32[16,8192]{1,0:T(8,128)S(1)}, f32[16,8192]{1,0:T(8,128)}, u32[]{:S(2)}, u32[]{:S(2)}) collective-permute-start(f32[16,8192]{1,0:T(8,128)S(1)} %get-tuple-element.948), channel_id=1, source_target_pairs={{8,0},{16,8},{24,16},{9,1},{17,9},{25,17},{10,2},{18,10},{26,18},{... | collective-permute-start | bytes 1572872 | tf_op jit(solution)/shard_map/ppermute | solution.py:14
  352.5 0.8 copy-start.8
  367.9 0.7 copy-start.2
  454.9 14.0 %collective-permute-start.6 = (f32[16,8192]{1,0:T(8,128)S(1)}, f32[16,8192]{1,0:T(8,128)S(1)}, u32[]{:S(2)}, u32[]{:S(2)}) collective-permute-start(f32[16,8192]{1,0:T(8,128)S(1)} %get-tuple-element.943), channel_id=1, source_target_pairs={{0,8},{8,16},{16,24},{1,9},{9,17},{17,25},{2,10},{10,18},{18,26},{... | collective-permute-start | bytes 1572872 | tf_op jit(solution)/shard_map/ppermute | solution.py:14
  457.3 15.8 %collective-permute-start.7 = (f32[16,8192]{1,0:T(8,128)S(1)}, f32[16,8192]{1,0:T(8,128)S(1)}, u32[]{:S(2)}, u32[]{:S(2)}) collective-permute-start(f32[16,8192]{1,0:T(8,128)S(1)} %get-tuple-element.944), channel_id=1, source_target_pairs={{8,0},{16,8},{24,16},{9,1},{17,9},{25,17},{10,2},{18,10},{26,18},{... | collective-permute-start | bytes 1572872 | tf_op jit(solution)/shard_map/ppermute | solution.py:14
